TPU v7x, 32 devices: a whole 2x2x4 slice. The times are simulated.
32 devices in a mesh: replica: 2 (over x), owner: 4 (over z), tensor: 4 (over y, core).
Axes of the slice: x: 2, y: 2, z: 4, core: 2. Of those that a mesh axis runs over, the one named last changes fastest.
Arguments:
- context: bfloat16 [4096, 8192], P(('replica', 'owner'), 'tensor'), parts along dimension 0, may hold values from -6 to 6
- output_weight: bfloat16 [8192, 8192], P('tensor'), may hold values from -0.09375 to 0.09375
- adapter_down: bfloat16 [64, 8192, 64], P('owner', 'tensor'), may hold values from -0.0625 to 0.0625
- adapter_up: bfloat16 [64, 64, 8192], P('owner', None, 'tensor'), may hold values from -0.75 to 0.75
- token_adapter: int32 [4096], P(('replica', 'owner')), parts along dimension 0, may hold values from 0 to 63, as said below
Outputs:
- projected: bfloat16 [4096, 8192], P(('replica', 'owner'), 'tensor'), parts along dimension 0
There are 2 independent parts, one for each index of `replica`. A program takes and returns all parts, laid end to end along the dimension named above; an argument that names none is the same for every part. Nothing has to cross between parts.
Inputs may be any that keep to these rules, and one draw needn't show every extreme that they name: `token_adapter`: adapter a belongs to owner a // 16. In each owner index's block of 512 consecutive tokens at most 256 tokens name adapters of one owner; one owner, the same for all blocks of a draw, is named by exactly 256 tokens of every block.
All inputs are finite; a program needn't handle non-finite values.
Results may differ from a plain program's by a relative error of at most 0.013.
Values may be sent and summed in bfloat16 or wider, within the bound.
A program may use at most 256 MiB of HBM per device.

v0:
```python
import jax
import jax.numpy as jnp
from jax import lax
from jax.sharding import PartitionSpec as P


def rank_total(partial_rank):
    return lax.psum(partial_rank.astype(jnp.bfloat16), "tensor").astype(jnp.float32)


def on_device(context, output_weight, adapter_down, adapter_up, token_adapter):
    owners = lax.axis_size("owner")
    tok_rows, feature_columns = context.shape
    per_adapter = adapter_down.shape[0]
    rank_extent = adapter_down.shape[2]
    partial_out = jnp.dot(context, output_weight, preferred_element_type=jnp.float32)
    output_sum = lax.psum_scatter(
        partial_out.astype(jnp.bfloat16), "tensor", scatter_dimension=1, tiled=True
    ).astype(jnp.float32)
    capacity = tok_rows // 2
    target = token_adapter // per_adapter
    within = token_adapter % per_adapter
    onehot = (target[:, None] == jnp.arange(owners)[None, :]).astype(jnp.int32)
    running_rank = jnp.cumsum(onehot, axis=0) - onehot
    position = jnp.sum(running_rank * onehot, axis=1)
    adapter_index = target * capacity + position
    outgoing = (
        jnp.zeros((owners * capacity, feature_columns), context.dtype)
        .at[adapter_index]
        .set(context)
    )
    outgoing_ids = jnp.full((owners * capacity,), -1, jnp.int32).at[adapter_index].set(within)
    arrived, arrived_ids = (
        lax.all_to_all(
            outgoing.reshape(owners, capacity, feature_columns),
            "owner",
            split_axis=0,
            concat_axis=0,
            tiled=True,
        ),
        lax.all_to_all(
            outgoing_ids.reshape(owners, capacity), "owner", split_axis=0, concat_axis=0, tiled=True
        ),
    )
    arrived = arrived.reshape(-1, feature_columns)
    arrived_ids = arrived_ids.reshape(-1)
    sort_keys = jnp.where(arrived_ids < 0, per_adapter, arrived_ids)
    ordering = jnp.argsort(sort_keys, stable=True)
    sorted_rows = arrived[ordering]
    group_sizes = jnp.sum(
        (sort_keys[:, None] == jnp.arange(per_adapter + 1)[None, :]).astype(jnp.int32), axis=0
    )
    padded_down = jnp.concatenate(
        [adapter_down, jnp.zeros((1, feature_columns, rank_extent), adapter_down.dtype)], axis=0
    )
    reduced = lax.ragged_dot(
        sorted_rows, padded_down, group_sizes, preferred_element_type=jnp.float32
    )
    reduced = rank_total(reduced).astype(jnp.bfloat16)
    padded_up = jnp.concatenate(
        [adapter_up, jnp.zeros((1, rank_extent, feature_columns), adapter_up.dtype)], axis=0
    )
    lifted_sorted = lax.ragged_dot(
        reduced, padded_up, group_sizes, preferred_element_type=jnp.float32
    ).astype(jnp.bfloat16)
    lifted = jnp.zeros_like(lifted_sorted).at[ordering].set(lifted_sorted)
    final_output = lax.all_to_all(
        lifted.reshape(owners, capacity, feature_columns),
        "owner",
        split_axis=0,
        concat_axis=0,
        tiled=True,
    )
    adapter_terms = final_output.reshape(-1, feature_columns)[adapter_index]
    return (output_sum + adapter_terms.astype(jnp.float32)).astype(jnp.bfloat16)


def solution(mesh):
    placed = (
        P(("replica", "owner"), "tensor"),
        P("tensor", None),
        P("owner", "tensor", None),
        P("owner", None, "tensor"),
        P(("replica", "owner")),
    )
    return jax.shard_map(
        on_device,
        mesh=mesh,
        in_specs=placed,
        out_specs=P(("replica", "owner"), "tensor"),
        check_vma=False,
    )
```

profile of v0, /device:TPU:8, one launch (start us, length us, event | category | flops | bytes accessed | tf_op | source)
XLA Modules:
  0.0 327.7 jit_solution(4808674215593662004)
XLA Ops:
  6.5 0.7 add_select_fusion
  7.2 1.2 reduce-window.6
  9.0 3.0 scatter_custom_fusion
  12.0 5.3 %all-to-all-start = ((s32[4,1,256]{2,1,0:T(1,128)}), s32[4,1,256]{2,1,0:T(1,128)S(1)}, u32[]{:S(2)}, u32[]{:S(2)}) async-start(s32[4,1,256]{2,1,0:T(1,128)} %bitcast.2), calls=%async_computation.1 | async-start | bytes 8192 | tf_op jit(solution)/shard_map/all_to_all | solution.py:41
  17.3 7.3 %scatter_custom_fusion.1 = bf16[1024,2048]{1,0:T(8,128)(2,1)} fusion(s32[512]{0:T(512)S(1)} %compare_select_fusion.2, bf16[512,2048]{1,0:T(8,128)(2,1)} %param.5, bf16[]{:T(256)} %constant.36.clone.1), kind=kCustom, calls=%fused_computation.10 | custom fusion | bytes 4194816 | tf_op jit(solution)/shard_map/scatter | solution.py:30
  24.6 5.1 %all-to-all-start.1 = ((bf16[4,256,2048]{2,1,0:T(8,128)(2,1)}), bf16[4,256,2048]{2,1,0:T(8,128)(2,1)}, u32[]{:S(2)}, u32[]{:S(2)}) async-start(bf16[4,256,2048]{2,1,0:T(8,128)(2,1)} %bitcast.28), calls=%async_computation.2 | async-start | bytes 8388608 | tf_op jit(solution)/shard_map/all_to_all | solution.py:34
  29.7 8.4 %copy.8 = bf16[16,2048,64]{2,1,0:T(8,128)(2,1)} copy(bf16[16,2048,64]{1,2,0:T(8,128)(2,1)} %param.7) | data formatting | bytes 8388608 | tf_op args[2]
  38.1 9.2 %concatenate.6 = bf16[17,2048,64]{2,1,0:T(8,128)(2,1)} pad(bf16[16,2048,64]{2,1,0:T(8,128)(2,1)} %copy.8, bf16[]{:T(256)} %constant.36.clone.1), padding=0_1x0_0x0_0 | pad | bytes 8650754 | tf_op jit(solution)/shard_map/concatenate | solution.py:53
  47.3 4.4 %sort.17 = (s32[1024]{0:T(1024)}, s32[1024]{0:T(1024)S(1)}) sort(s32[1024]{0:T(1024)S(1)} %compare_select_fusion.1, s32[1024]{0:T(1024)S(1)} %iota.16), dimensions={0}, to_apply=%region_5.6 | sort | flops 10240 | bytes 16384 | tf_op jit(solution)/shard_map/jit(argsort)/sort | solution.py:48
  51.7 0.6 convert_reduce_fusion
  52.3 1.8 ragged-dot-metadata
  54.1 65.1 %all-to-all-done.1 = bf16[4,256,2048]{2,1,0:T(8,128)(2,1)} async-done(((bf16[4,256,2048]{2,1,0:T(8,128)(2,1)}), bf16[4,256,2048]{2,1,0:T(8,128)(2,1)}, u32[]{:S(2)}, u32[]{:S(2)}) %all-to-all-start.1) | async-done | bytes 4194336 | tf_op jit(solution)/shard_map/all_to_all | solution.py:34
  119.3 11.6 %gather_fusion = bf16[1024,2048]{1,0:T(8,128)(2,1)} fusion(bf16[1024,2048]{1,0:T(8,128)(2,1)} %bitcast.5, s32[1024]{0:T(1024)S(1)} %get-tuple-element.15), kind=kCustom, calls=%fused_computation | custom fusion | bytes 8392704 | tf_op jit(solution)/shard_map/gather | solution.py:49
  130.8 19.0 %ragged-dot-none.1 = f32[1024,64]{1,0:T(8,128)} custom-call(s32[1]{0:T(128)} %get-tuple-element.7, s32[18]{0:T(128)} %get-tuple-element.8, s32[20]{0:T(128)} %get-tuple-element.9, s32[20]{0:T(128)} %get-tuple-element.10, s32[1]{0:T(128)} %get-tuple-element.7, bf16[1024,2048]{1,0:T(8,128)(2,1)} %gather_fusion, bf16[17,2048,64]{2,1,0:T(8,128)(2,1)} %concatenate.6), custom_call_target="tpu_custom_call" | custom-call | flops 268435456 | bytes 8912964 | tf_op jit(solution)/shard_map/ragged_dot_general/ragged-dot-none
  149.9 1.8 convert_element_type.35
  151.9 25.5 %convolution_convert_fusion = bf16[512,8192]{1,0:T(8,128)(2,1)} fusion(bf16[512,2048]{1,0:T(8,128)(2,1)S(1)} %copy-done, bf16[2048,8192]{1,0:T(8,128)(2,1)} %param.6), kind=kOutput, calls=%fused_computation.5 | convolution fusion | flops 17184063488 | bytes 44040192 | tf_op jit(solution)/shard_map/dot_general | solution.py:16
  177.4 4.8 %concatenate.7 = bf16[17,64,2048]{2,1,0:T(8,128)(2,1)} pad(bf16[16,64,2048]{2,1,0:T(8,128)(2,1)} %param.8, bf16[]{:T(256)} %constant.36.clone.1), padding=0_1x0_0x0_0 | pad | bytes 8650754 | tf_op jit(solution)/shard_map/concatenate | solution.py:60
  182.2 3.6 %all-reduce.4.cloned.1.call-done = bf16[1024,64]{1,0:T(8,128)(2,1)} async-done(((bf16[1024,64]{1,0:T(8,128)(2,1)}), bf16[1024,64]{1,0:T(8,128)(2,1)}) %all-reduce.4.cloned.1.call-update) | async-done | bytes 131088 | tf_op jit(solution)/shard_map/psum | solution.py:8
  185.9 18.6 %ragged-dot-none = f32[1024,2048]{1,0:T(8,128)} custom-call(s32[1]{0:T(128)} %get-tuple-element.7, s32[18]{0:T(128)} %get-tuple-element.8, s32[20]{0:T(128)} %get-tuple-element.9, s32[20]{0:T(128)} %get-tuple-element.10, s32[1]{0:T(128)} %get-tuple-element.7, bf16[1024,64]{1,0:T(8,128)(2,1)} %all-reduce.4.cloned.1.call-done, bf16[17,64,2048]{2,1,0:T(8,128)(2,1)} %concatenate.7), custom_call_target="tpu_custom_call" | custom-call | flops 268435456 | bytes 12976196 | tf_op jit(solution)/shard_map/ragged_dot_general/ragged-dot-none
  204.5 10.6 %scatter_custom_fusion.2 = bf16[1024,2048]{1,0:T(8,128)(2,1)} fusion(s32[1024]{0:T(1024)S(1)} %get-tuple-element.16, f32[1024,2048]{1,0:T(8,128)} %ragged-dot-none, bf16[]{:T(256)} %constant.36.clone.1), kind=kCustom, calls=%fused_computation.7 | custom fusion | flops 2097152 | bytes 12582914 | tf_op jit(solution)/shard_map/scatter | solution.py:66
  215.1 5.6 %all-to-all-start.2 = ((bf16[4,256,2048]{2,1,0:T(8,128)(2,1)}), bf16[4,256,2048]{2,1,0:T(8,128)(2,1)}, u32[]{:S(2)}, u32[]{:S(2)}) async-start(bf16[4,256,2048]{2,1,0:T(8,128)(2,1)} %bitcast.29), calls=%async_computation.3 | async-start | bytes 8388608 | tf_op jit(solution)/shard_map/all_to_all | solution.py:67
  220.7 89.3 %all-to-all-done.2 = bf16[4,256,2048]{2,1,0:T(8,128)(2,1)} async-done(((bf16[4,256,2048]{2,1,0:T(8,128)(2,1)}), bf16[4,256,2048]{2,1,0:T(8,128)(2,1)}, u32[]{:S(2)}, u32[]{:S(2)}) %all-to-all-start.2) | async-done | bytes 4194336 | tf_op jit(solution)/shard_map/all_to_all | solution.py:67
  310.0 7.1 %gather_fusion.1 = bf16[512,2048]{1,0:T(8,128)(2,1)S(1)} fusion(bf16[1024,2048]{1,0:T(8,128)(2,1)} %bitcast.7, s32[1024]{0:T(1024)S(1)} %pad_clamp_fusion), kind=kCustom, calls=%fused_computation.1 | custom fusion | bytes 4196352 | tf_op jit(solution)/shard_map/gather | solution.py:74
  317.2 3.7 %add_convert_fusion = bf16[512,2048]{1,0:T(8,128)(2,1)} fusion(bf16[512,2048]{1,0:T(8,128)(2,1)S(1)} %gather_fusion.1, bf16[512,2048]{1,0:T(8,128)(2,1)} %reduce-scatter.2.cloned.1.call-done), kind=kLoop, calls=%fused_computation.6 | loop fusion | flops 4194304 | bytes 6291456 | tf_op jit(solution)/shard_map/convert_element_type | solution.py:75
  (18 shorter events, 0.8 us)
Async XLA Ops:
  12.0 12.6 %all-to-all-start = ((s32[4,1,256]{2,1,0:T(1,128)}), s32[4,1,256]{2,1,0:T(1,128)S(1)}, u32[]{:S(2)}, u32[]{:S(2)}) async-start(s32[4,1,256]{2,1,0:T(1,128)} %bitcast.2), calls=%async_computation.1 | async-start | bytes 8192 | tf_op jit(solution)/shard_map/all_to_all | solution.py:41
  24.6 94.7 %all-to-all-start.1 = ((bf16[4,256,2048]{2,1,0:T(8,128)(2,1)}), bf16[4,256,2048]{2,1,0:T(8,128)(2,1)}, u32[]{:S(2)}, u32[]{:S(2)}) async-start(bf16[4,256,2048]{2,1,0:T(8,128)(2,1)} %bitcast.28), calls=%async_computation.2 | async-start | bytes 8388608 | tf_op jit(solution)/shard_map/all_to_all | solution.py:34
  29.7 156.2 %all-reduce.4.cloned.1.call-start = ((), (), s32[]{:S(2)}) async-start(), calls=%async_computation.5 | async-start | bytes 524288 | tf_op jit(solution)/shard_map/psum | solution.py:8
  130.8 21.1 %copy-start = (bf16[512,2048]{1,0:T(8,128)(2,1)S(1)}, bf16[512,2048]{1,0:T(8,128)(2,1)}, u32[]{:S(2)}) copy-start(bf16[512,2048]{1,0:T(8,128)(2,1)} %param.5) | copy-start | bytes 6291460
  151.7 165.5 %reduce-scatter.2.cloned.1.call-start = ((), (), s32[]{:S(2)}) async-start(), calls=%async_computation.4 | async-start | bytes 10485760 | tf_op jit(solution)/shard_map/reduce_scatter | solution.py:17
  215.1 94.9 %all-to-all-start.2 = ((bf16[4,256,2048]{2,1,0:T(8,128)(2,1)}), bf16[4,256,2048]{2,1,0:T(8,128)(2,1)}, u32[]{:S(2)}, u32[]{:S(2)}) async-start(bf16[4,256,2048]{2,1,0:T(8,128)(2,1)} %bitcast.29), calls=%async_computation.3 | async-start | bytes 8388608 | tf_op jit(solution)/shard_map/all_to_all | solution.py:67
Sparse Core Ops, SparseCore 0:
  151.8 34.0 all-reduce.3
  188.6 71.7 reduce-scatter.1
where the time goes:
time: 333 us; the launch traced here: 328 us
  waiting for transfers between devices  158 us (47%)
  local copies, waits for them, and re-layouts  51.6 us (15%)
  Pallas kernels  39.5 us (12%)
  matrix products  25.5 us (8%)
  other arithmetic  23.3 us (7%)
  starting transfers between devices  16.2 us (5%)
  between operations  13.5 us (4%)
    all_to_all x1, waiting for transfers between devices, on_device(): lax.all_to_all(lifted.reshape(owners, capacity, feature_columns), 'owner'...  89.3 us
    all_to_all x1, waiting for transfers between devices, on_device(): lax.all_to_all(outgoing.reshape(owners, capacity, feature_columns), 'owne...  65.1 us
    another operation x2, Pallas kernels  37.6 us
    dot_general x1, matrix products, on_device(): jnp.dot(context, output_weight, preferred_element_type=jnp.float32)  25.5 us
    gather x1, local copies, waits for them, and re-layouts, on_device(): sorted_rows = arrived[ordering]  11.6 us
    scatter x1, other arithmetic, on_device(): lifted = jnp.zeros_like(lifted_sorted).at[ordering].set(lifted_sorted)  10.6 us
    concatenate x1, local copies, waits for them, and re-layouts, on_device(): jnp.concatenate([adapter_down, jnp.zeros((1, feature_columns, rank_extent...  9.15 us
    unnamed x3, local copies, waits for them, and re-layouts  8.44 us
  transfers between devices with their start and end apart: 5, of which 3 were waited for; matrix products, arithmetic and copies ran while one was open for 24% of the time, Pallas kernels for 6%

commit v1 on v0

v1 whole, which is shorter than its diff:
```python
import jax
import jax.numpy as jnp
from jax import lax
from jax.sharding import PartitionSpec as P

BF16 = jnp.bfloat16
F32 = jnp.float32


def rank_in_owner(ids, per_adapter, owners):
    tokens = ids.shape[1]
    target = ids // per_adapter
    onehot = (target[:, :, None] == jnp.arange(owners)[None, None, :]).astype(BF16)
    before = (jnp.arange(tokens)[:, None] > jnp.arange(tokens)[None, :]).astype(BF16)
    counts = jnp.einsum("tu,buo->bto", before, onehot, preferred_element_type=F32)
    rank = jnp.sum(counts * onehot.astype(F32), axis=2).astype(jnp.int32)
    return target, rank


def on_device(context, output_weight, adapter_down, adapter_up, token_adapter):
    owners = lax.axis_size("owner")
    me = lax.axis_index("owner")
    tokens, features = context.shape
    per_adapter, _, rank_extent = adapter_down.shape
    capacity = tokens // 2
    chunks = 2
    slots = capacity // chunks
    wide = per_adapter * rank_extent

    all_ids = lax.all_gather(token_adapter, "owner", axis=0, tiled=False)
    target, rank = rank_in_owner(token_adapter[None], per_adapter, owners)
    target, rank = target[0], rank[0]

    places, sent = [], []
    for chunk in range(chunks):
        slot = jnp.where(rank // slots == chunk, target * slots + rank % slots, -1)
        place = (slot[:, None] == jnp.arange(owners * slots)[None, :]).astype(BF16)
        outgoing = lax.dot_general(
            place, context, (((0,), (0,)), ((), ())), preferred_element_type=F32
        ).astype(BF16)
        arrived = lax.all_to_all(
            outgoing.reshape(owners, slots, features), "owner", 0, 0, tiled=True
        ).reshape(owners * slots, features)
        places.append(place)
        sent.append(arrived)

    partial_out = jnp.dot(context, output_weight, preferred_element_type=F32).astype(BF16)
    output_sum = lax.psum_scatter(partial_out, "tensor", scatter_dimension=1, tiled=True)

    down = adapter_down.transpose(1, 0, 2).reshape(features, wide)
    up = adapter_up.reshape(wide, features)
    pick = (
        jnp.arange(wide)[:, None] % rank_extent == jnp.arange(rank_extent)[None, :]
    ).astype(BF16)
    block_of = jnp.arange(wide)[None, :] // rank_extent

    all_target, all_rank = rank_in_owner(all_ids, per_adapter, owners)
    all_within = jnp.where(all_target == me, all_ids % per_adapter, -1)

    back = []
    for chunk in range(chunks):
        here = all_rank[:, :, None] == (chunk * slots + jnp.arange(slots))[None, None, :]
        ids = jnp.max(jnp.where(here, all_within[:, :, None], -1), axis=1).reshape(-1)
        mask = ids[:, None] == block_of
        full = jnp.dot(sent[chunk], down, preferred_element_type=F32)
        full = jnp.where(mask, full, 0.0).astype(BF16)
        partial_rank = jnp.dot(full, pick, preferred_element_type=F32).astype(BF16)
        reduced = lax.psum(partial_rank, "tensor")
        spread = lax.dot_general(
            reduced, pick, (((1,), (1,)), ((), ())), preferred_element_type=F32
        )
        spread = jnp.where(mask, spread, 0.0).astype(BF16)
        lifted = jnp.dot(spread, up, preferred_element_type=F32).astype(BF16)
        back.append(
            lax.all_to_all(
                lifted.reshape(owners, slots, features), "owner", 0, 0, tiled=True
            ).reshape(owners * slots, features)
        )

    total = output_sum.astype(F32)
    for chunk in range(chunks):
        total = total + jnp.dot(places[chunk], back[chunk], preferred_element_type=F32)
    return total.astype(BF16)


def solution(mesh):
    placed = (
        P(("replica", "owner"), "tensor"),
        P("tensor", None),
        P("owner", "tensor", None),
        P("owner", None, "tensor"),
        P(("replica", "owner")),
    )
    return jax.shard_map(
        on_device,
        mesh=mesh,
        in_specs=placed,
        out_specs=P(("replica", "owner"), "tensor"),
        check_vma=False,
    )
```

time: 333 us -> 291 us (0.87)
  local copies, waits for them, and re-layouts: 51.6 us -> 0.02 us
  blocking collectives: 0 us -> 48.8 us
  matrix products: 25.5 us -> 66.7 us
  Pallas kernels: 39.5 us -> 0 us
  waiting for transfers between devices: 158 us -> 128 us
  other arithmetic: 23.3 us -> 2.3 us
  starting transfers between devices: 16.2 us -> 26.4 us
    all_gather x0 -> x1, blocking collectives: none -> 48.8 us  [on_device(): all_ids = lax.all_gather(token_adapter, 'owner', axis=0, tiled=False)]
    dot_general x1 -> x11, matrix products: 25.5 us -> 66.7 us  [the longest x1 25.4 us: on_device(): jnp.dot(context, output_weight, preferred_element_type=F32).astype(BF16)]
    another operation x2 -> x0, Pallas kernels: 37.6 us -> none
    all_to_all x3 -> x4, waiting for transfers between devices: 154 us -> 120 us  [the longest x2 77.9 us: on_device(): lax.all_to_all(lifted.reshape(owners, slots, features), 'owner', 0, 0, ti...]
    gather x2 -> x0, local copies, waits for them, and re-layouts: 18.7 us -> none  [the longest x1 11.6 us: on_device(): sorted_rows = arrived[ordering]]
    concatenate x2 -> x0, local copies, waits for them, and re-layouts: 14 us -> none  [the longest x1 9.15 us: on_device(): jnp.concatenate([adapter_down, jnp.zeros((1, feature_columns, rank_extent...]
    scatter x1 -> x0, other arithmetic: 10.6 us -> none  [on_device(): lifted = jnp.zeros_like(lifted_sorted).at[ordering].set(lifted_sorted)]
    scatter x2 -> x0, local copies, waits for them, and re-layouts: 10.3 us -> none  [the longest x1 7.3 us: on_device(): outgoing = jnp.zeros((owners * capacity, feature_columns), context.dtype)...]
  transfers between devices with their start and end apart: 5 -> 6, of which waited for: 3 -> 4; matrix products, arithmetic and copies ran while one was open for 24% -> 18% of each run, Pallas kernels for 6% -> 0%
where the time goes in v1:
time: 291 us; the launch traced here: 286 us
  waiting for transfers between devices  128 us (44%)
  matrix products  66.7 us (23%)
  blocking collectives  48.8 us (17%)
  starting transfers between devices  26.4 us (9%)
  between operations  13.5 us (5%)
    all_to_all x2, waiting for transfers between devices, on_device(): lax.all_to_all(lifted.reshape(owners, slots, features), 'owner', 0, 0, ti...  77.9 us
    all_gather x1, blocking collectives, on_device(): all_ids = lax.all_gather(token_adapter, 'owner', axis=0, tiled=False)  48.8 us
    all_to_all x2, waiting for transfers between devices, on_device(): lax.all_to_all(outgoing.reshape(owners, slots, features), 'owner', 0, 0,...  42.2 us
    dot_general x1, matrix products, on_device(): jnp.dot(context, output_weight, preferred_element_type=F32).astype(BF16)  25.4 us
    dot_general x2, matrix products, on_device(): lifted = jnp.dot(spread, up, preferred_element_type=F32).astype(BF16)  13.5 us
    all_to_all x2, starting transfers between devices, on_device(): lax.all_to_all(outgoing.reshape(owners, slots, features), 'owner', 0, 0,...  13.2 us
    all_to_all x2, starting transfers between devices, on_device(): lax.all_to_all(lifted.reshape(owners, slots, features), 'owner', 0, 0, ti...  13 us
    dot_general x2, matrix products, on_device(): partial_rank = jnp.dot(full, pick, preferred_element_type=F32).astype(BF16)  12.2 us
  transfers between devices with their start and end apart: 6, of which 4 were waited for; matrix products, arithmetic and copies ran while one was open for 18% of the time, Pallas kernels for 0%

profile of v1, /device:TPU:8, one launch (start us, length us, event | category | flops | bytes accessed | tf_op | source)
XLA Modules:
  0.0 285.7 jit_solution(15006059024027526202)
XLA Ops:
  6.5 0.8 add_select_fusion.5
  7.4 0.4 fusion.11
  7.8 0.7 compare_select_fusion.4
  8.5 2.7 convolution_convert_fusion.4
  11.2 5.3 %all-to-all-start = ((bf16[4,128,2048]{2,1,0:T(8,128)(2,1)}), bf16[4,128,2048]{2,1,0:T(8,128)(2,1)}, u32[]{:S(2)}, u32[]{:S(2)}) async-start(bf16[4,128,2048]{2,1,0:T(8,128)(2,1)} %bitcast.73), calls=%async_computation.1 | async-start | bytes 4194304 | tf_op jit(solution)/shard_map/all_to_all | solution.py:41
  16.5 2.7 convolution_convert_fusion.3
  19.2 42.2 %all-to-all-done = bf16[4,128,2048]{2,1,0:T(8,128)(2,1)} async-done(((bf16[4,128,2048]{2,1,0:T(8,128)(2,1)}), bf16[4,128,2048]{2,1,0:T(8,128)(2,1)}, u32[]{:S(2)}, u32[]{:S(2)}) %all-to-all-start) | async-done | bytes 2097184 | tf_op jit(solution)/shard_map/all_to_all | solution.py:41
  61.4 7.9 %all-to-all-start.2 = ((bf16[4,128,2048]{2,1,0:T(8,128)(2,1)}), bf16[4,128,2048]{2,1,0:T(8,128)(2,1)}, u32[]{:S(2)}, u32[]{:S(2)}) async-start(bf16[4,128,2048]{2,1,0:T(8,128)(2,1)} %bitcast.70), calls=%async_computation.3 | async-start | bytes 4194304 | tf_op jit(solution)/shard_map/all_to_all | solution.py:41
  69.3 48.8 %all-gather.1 = s32[4,1,512]{2,1,0:T(1,128)S(1)} all-gather(s32[1,1,512]{2,1,0:T(1,128)S(1)} %bitcast.74), channel_id=2, replica_groups=mesh['replica'=2,'owner'=4,'tensor'=4] {'owner'}, dimensions={0}, use_global_device_ids=true | all-gather | bytes 10240 | tf_op jit(solution)/shard_map/all_gather | solution.py:30
  118.2 0.3 fusion.9
  118.5 0.7 select_reduce_fusion
  119.2 6.1 %fusion.6 = bf16[512,64]{0,1:T(8,128)(2,1)} fusion(bf16[512,2048]{1,0:T(8,128)(2,1)} %bitcast.7, bf16[2048,1024]{0,1:T(8,128)(2,1)} %bitcast.79, s32[1024]{0:T(1024)S(1)} %get-tuple-element.14, s32[512]{0:T(512)S(1)} %bitcast.77, s32[1024]{0:T(1024)S(1)} %get-tuple-element.13), kind=kOutput, calls=%fused_computation.16 | convolution fusion | flops 2216263680 | bytes 6367232 | tf_op jit(solution)/shard_map/dot_general | solution.py:67
  125.3 6.1 %fusion.7 = bf16[512,64]{0,1:T(8,128)(2,1)} fusion(bf16[512,2048]{1,0:T(8,128)(2,1)} %bitcast.15, bf16[2048,1024]{0,1:T(8,128)(2,1)} %bitcast.80, s32[1024]{0:T(1024)S(1)} %get-tuple-element.14, s32[512]{0:T(512)S(1)} %bitcast.75, s32[1024]{0:T(1024)S(1)} %get-tuple-element.13), kind=kOutput, calls=%fused_computation.17 | convolution fusion | flops 2216263680 | bytes 6367232 | tf_op jit(solution)/shard_map/dot_general | solution.py:67
  131.4 0.2 reduce-scatter.2.cloned.1.call-start
  131.6 25.4 %convolution_convert_fusion = bf16[512,8192]{1,0:T(8,128)(2,1)} fusion(bf16[512,2048]{1,0:T(8,128)(2,1)S(1)} %copy-done, bf16[2048,8192]{1,0:T(8,128)(2,1)} %param.6), kind=kOutput, calls=%fused_computation | convolution fusion | flops 17184063488 | bytes 44040192 | tf_op jit(solution)/shard_map/dot_general | solution.py:47
  157.1 7.8 %all-reduce.3.cloned.1.call-done = (bf16[512,64]{0,1:T(8,128)(2,1)}, bf16[512,64]{0,1:T(8,128)(2,1)}) async-done(((bf16[512,64]{0,1:T(8,128)(2,1)}, bf16[512,64]{0,1:T(8,128)(2,1)}), (bf16[512,64]{0,1:T(8,128)(2,1)}, bf16[512,64]{0,1:T(8,128)(2,1)})) %all-reduce.3.cloned.1.call-update) | async-done | bytes 131088 | tf_op jit(solution)/shard_map/psum | solution.py:68
  164.9 6.4 %convolution_convert_fusion.2 = bf16[512,2048]{1,0:T(8,128)(2,1)} fusion(bf16[1024,2048]{1,0:T(8,128)(2,1)} %bitcast.81, bf16[512,64]{0,1:T(8,128)(2,1)} %get-tuple-element.7, s32[1024]{0:T(1024)S(1)} %get-tuple-element.14, s32[512]{0:T(512)S(1)} %bitcast.78, s32[1024]{0:T(1024)S(1)} %get-tuple-element.13), kind=kOutput, calls=%fused_computation.3 | convolution fusion | flops 2217279488 | bytes 6367232 | tf_op jit(solution)/shard_map/dot_general | solution.py:73
  171.3 5.3 %all-to-all-start.1 = ((bf16[4,128,2048]{2,1,0:T(8,128)(2,1)}), bf16[4,128,2048]{2,1,0:T(8,128)(2,1)S(1)}, u32[]{:S(2)}, u32[]{:S(2)}) async-start(bf16[4,128,2048]{2,1,0:T(8,128)(2,1)} %bitcast.72), calls=%async_computation.2 | async-start | bytes 4194304 | tf_op jit(solution)/shard_map/all_to_all | solution.py:75
  176.6 7.2 %convolution_convert_fusion.1 = bf16[512,2048]{1,0:T(8,128)(2,1)} fusion(bf16[1024,2048]{1,0:T(8,128)(2,1)} %bitcast.82, bf16[512,64]{0,1:T(8,128)(2,1)S(1)} %copy-done.3, s32[1024]{0:T(1024)S(1)} %get-tuple-element.14, s32[512]{0:T(512)S(1)} %bitcast.76, s32[1024]{0:T(1024)S(1)} %get-tuple-element.13), kind=kOutput, calls=%fused_computation.2 | convolution fusion | flops 2217279488 | bytes 6367232 | tf_op jit(solution)/shard_map/dot_general | solution.py:73
  183.7 36.7 %all-to-all-done.1 = bf16[4,128,2048]{2,1,0:T(8,128)(2,1)S(1)} async-done(((bf16[4,128,2048]{2,1,0:T(8,128)(2,1)}), bf16[4,128,2048]{2,1,0:T(8,128)(2,1)S(1)}, u32[]{:S(2)}, u32[]{:S(2)}) %all-to-all-start.1) | async-done | bytes 2097184 | tf_op jit(solution)/shard_map/all_to_all | solution.py:75
  220.5 7.7 %all-to-all-start.3 = ((bf16[4,128,2048]{2,1,0:T(8,128)(2,1)}), bf16[4,128,2048]{2,1,0:T(8,128)(2,1)}, u32[]{:S(2)}, u32[]{:S(2)}) async-start(bf16[4,128,2048]{2,1,0:T(8,128)(2,1)} %bitcast.71), calls=%async_computation.4 | async-start | bytes 4194304 | tf_op jit(solution)/shard_map/all_to_all | solution.py:75
  228.2 3.3 %fusion.20 = f32[512,2048]{1,0:T(8,128)} fusion(bf16[512,2048]{1,0:T(8,128)(2,1)S(1)} %bitcast.69, s32[512]{0:T(512)S(1)} %get-tuple-element.12), kind=kOutput, calls=%fused_computation.37 | convolution fusion | flops 1074003968 | bytes 6293504 | tf_op jit(solution)/shard_map/dot_general | solution.py:82
  231.4 41.1 %all-to-all-done.3 = bf16[4,128,2048]{2,1,0:T(8,128)(2,1)} async-done(((bf16[4,128,2048]{2,1,0:T(8,128)(2,1)}), bf16[4,128,2048]{2,1,0:T(8,128)(2,1)}, u32[]{:S(2)}, u32[]{:S(2)}) %all-to-all-start.3) | async-done | bytes 2097184 | tf_op jit(solution)/shard_map/all_to_all | solution.py:75
  272.6 6.2 %add_convert_fusion = bf16[512,2048]{1,0:T(8,128)(2,1)} fusion(f32[512,2048]{1,0:T(8,128)} %fusion.20, bf16[512,2048]{1,0:T(8,128)(2,1)} %reduce-scatter.2.cloned.1.call-done, bf16[512,2048]{1,0:T(8,128)(2,1)} %bitcast.18, s32[512]{0:T(512)S(1)} %get-tuple-element.11), kind=kOutput, calls=%fused_computation.1 | convolution fusion | flops 1078198272 | bytes 10487808 | tf_op jit(solution)/shard_map/dot_general | solution.py:82
  (17 shorter events, 0.1 us)
Async XLA Ops:
  6.5 1.9 copy-start
  11.2 50.2 %all-to-all-start = ((bf16[4,128,2048]{2,1,0:T(8,128)(2,1)}), bf16[4,128,2048]{2,1,0:T(8,128)(2,1)}, u32[]{:S(2)}, u32[]{:S(2)}) async-start(bf16[4,128,2048]{2,1,0:T(8,128)(2,1)} %bitcast.73), calls=%async_computation.1 | async-start | bytes 4194304 | tf_op jit(solution)/shard_map/all_to_all | solution.py:41
  61.4 7.9 %copy-start.2 = (s32[512]{0:T(512)S(1)}, s32[512]{0:T(512)}, u32[]{:S(2)}) copy-start(s32[512]{0:T(512)} %param.9) | copy-start | bytes 6148
  61.4 63.9 %all-to-all-start.2 = ((bf16[4,128,2048]{2,1,0:T(8,128)(2,1)}), bf16[4,128,2048]{2,1,0:T(8,128)(2,1)}, u32[]{:S(2)}, u32[]{:S(2)}) async-start(bf16[4,128,2048]{2,1,0:T(8,128)(2,1)} %bitcast.70), calls=%async_computation.3 | async-start | bytes 4194304 | tf_op jit(solution)/shard_map/all_to_all | solution.py:41
  69.3 95.6 %all-reduce.3.cloned.1.call-start = ((), (), s32[]{:S(2)}) async-start(), calls=%async_computation.6 | async-start | bytes 262144 | tf_op jit(solution)/shard_map/psum | solution.py:68
  131.4 141.2 %reduce-scatter.2.cloned.1.call-start = ((), (), s32[]{:S(2)}) async-start(), calls=%async_computation.5 | async-start | bytes 10485760 | tf_op jit(solution)/shard_map/reduce_scatter | solution.py:48
  171.3 5.3 %copy-start.3 = (bf16[512,64]{0,1:T(8,128)(2,1)S(1)}, bf16[512,64]{0,1:T(8,128)(2,1)}, u32[]{:S(2)}) copy-start(bf16[512,64]{0,1:T(8,128)(2,1)} %get-tuple-element.8) | copy-start | bytes 196612
  171.3 49.2 %all-to-all-start.1 = ((bf16[4,128,2048]{2,1,0:T(8,128)(2,1)}), bf16[4,128,2048]{2,1,0:T(8,128)(2,1)S(1)}, u32[]{:S(2)}, u32[]{:S(2)}) async-start(bf16[4,128,2048]{2,1,0:T(8,128)(2,1)} %bitcast.72), calls=%async_computation.2 | async-start | bytes 4194304 | tf_op jit(solution)/shard_map/all_to_all | solution.py:75
  220.5 52.1 %all-to-all-start.3 = ((bf16[4,128,2048]{2,1,0:T(8,128)(2,1)}), bf16[4,128,2048]{2,1,0:T(8,128)(2,1)}, u32[]{:S(2)}, u32[]{:S(2)}) async-start(bf16[4,128,2048]{2,1,0:T(8,128)(2,1)} %bitcast.71), calls=%async_computation.4 | async-start | bytes 4194304 | tf_op jit(solution)/shard_map/all_to_all | solution.py:75
  272.6 6.2 %copy-start.1 = (bf16[512,2048]{1,0:T(8,128)(2,1)S(1)}, bf16[512,2048]{1,0:T(8,128)(2,1)}, u32[]{:S(2)}) copy-start(bf16[512,2048]{1,0:T(8,128)(2,1)} %param.5) | copy-start | bytes 6291460
Sparse Core Ops, SparseCore 0:
  131.5 33.3 all-reduce.2
  167.7 71.7 reduce-scatter.1

commit v2 on v0

v2 whole, which is shorter than its diff:
```python
import functools

import jax
import jax.numpy as jnp
from jax import lax
from jax.experimental import pallas as pl
from jax.experimental.pallas import tpu as pltpu
from jax.sharding import PartitionSpec as P

BF16 = jnp.bfloat16
F32 = jnp.float32
MESH = pl.DeviceIdType.MESH
CORES = 2
CHUNKS = 2


def remote(src, dst, send, recv, axis, index):
    return pltpu.make_async_remote_copy(
        src_ref=src,
        dst_ref=dst,
        send_sem=send,
        recv_sem=recv,
        device_id={axis: index},
        device_id_type=MESH,
    )


def kernel(
    owners,
    tensors,
    tile,
    ctx_ref,
    w_ref,
    down_ref,
    up_ref,
    outgoing_ref,
    ids_out_ref,
    place_ref,
    out_ref,
    arrived,
    ids_in,
    stage,
    down,
    up,
    wbuf,
    pair_out,
    pair_in,
    far_out,
    far_in,
    sib_out,
    sib_in,
    total,
    rank_out,
    rank_in,
    lifted,
    back,
    w_sem,
    stage_sem,
    local_sem,
    ids_send,
    ids_recv,
    out_send,
    out_recv,
    pair_send,
    pair_recv,
    far_send,
    far_recv,
    sib_send,
    sib_recv,
    rank_send,
    rank_recv,
    back_send,
    back_recv,
):
    me = lax.axis_index("owner")
    t = lax.axis_index("tensor")
    y, core = t // CORES, t % CORES
    chips = tensors // CORES
    sibling = y * CORES + 1 - core
    rows, features = ctx_ref.shape
    per_adapter, _, rank_extent = down_ref.shape
    wide = per_adapter * rank_extent
    slots = outgoing_ref.shape[2]
    block = owners * slots

    barrier = pltpu.get_barrier_semaphore()
    for d in range(1, owners):
        pl.semaphore_signal(
            barrier, inc=1, device_id={"owner": lax.rem(me + d, owners)}, device_id_type=MESH
        )
    for d in range(1, tensors):
        pl.semaphore_signal(
            barrier, inc=1, device_id={"tensor": lax.rem(t + d, tensors)}, device_id_type=MESH
        )
    pl.semaphore_wait(barrier, owners + tensors - 2)

    def ids_copy(d, at):
        to = lax.rem(me + d, owners)
        return remote(
            ids_out_ref.at[to], ids_in.at[at], ids_send.at[d - 1], ids_recv.at[d - 1], "owner", to
        )

    def rows_copy(c, d, at):
        to = lax.rem(me + d, owners)
        return remote(
            outgoing_ref.at[c, to],
            arrived.at[c, at],
            out_send.at[c, d - 1],
            out_recv.at[c, d - 1],
            "owner",
            to,
        )

    def back_copy(c, d, at):
        to = lax.rem(me + d, owners)
        return remote(
            lifted.at[c, to], back.at[c, at], back_send.at[c, d - 1], back_recv.at[c, d - 1], "owner", to
        )

    def source(d):
        return lax.rem(me - d + owners, owners)

    for d in range(1, owners):
        ids_copy(d, me).start()
    for c in range(CHUNKS):
        for d in range(1, owners):
            rows_copy(c, d, me).start()

    locals_ = [pltpu.make_async_copy(up_ref, up, local_sem.at[0])]
    locals_.append(pltpu.make_async_copy(ids_out_ref.at[me], ids_in.at[me], local_sem.at[1]))
    for c in range(CHUNKS):
        locals_.append(
            pltpu.make_async_copy(outgoing_ref.at[c, me], arrived.at[c, me], local_sem.at[2 + c])
        )
    for copy in locals_:
        copy.start()

    steps = features // tile
    others = [lax.rem(y + 1 + k, chips) for k in range(chips - 1)]
    order = [o * CORES + 1 - core for o in others]
    order += [o * CORES + core for o in others]
    order += [sibling, t]

    def fetch(column, slot):
        return pltpu.make_async_copy(
            w_ref.at[:, pl.ds(pl.multiple_of(column, tile), tile)], wbuf.at[slot], w_sem.at[slot]
        )

    def product(p, store):
        first = order[p] * features
        after = order[p + 1] * features if p + 1 < tensors else None

        def body(j, carry):
            slot = lax.rem(p * steps + j, 2)
            if after is not None:
                fetch(jnp.where(j + 1 < steps, first + (j + 1) * tile, after), 1 - slot).start()
            else:

                @pl.when(j + 1 < steps)
                def _():
                    fetch(first + (j + 1) * tile, 1 - slot).start()

            fetch(first + j * tile, slot).wait()
            store(
                pl.ds(pl.multiple_of(j * tile, tile), tile),
                jnp.dot(ctx_ref[...], wbuf[slot], preferred_element_type=F32).astype(BF16),
            )
            return carry

        lax.fori_loop(0, steps, body, 0)

    def pair_copy(k):
        return remote(
            pair_out.at[k], pair_in.at[k], pair_send.at[k], pair_recv.at[k], "tensor", sibling
        )

    def far_copy(k):
        return remote(
            far_out.at[k],
            far_in.at[k],
            far_send.at[k],
            far_recv.at[k],
            "tensor",
            others[k] * CORES + core,
        )

    def sib_copy():
        return remote(sib_out, sib_in, sib_send, sib_recv, "tensor", sibling)

    fetch(order[0] * features, 0).start()
    for k in range(chips - 1):

        def keep_pair(columns, value, k=k):
            pair_out[k, :, columns] = value

        product(k, keep_pair)
        pair_copy(k).start()
    for k in range(chips - 1):
        pair_copy(k).wait_recv()

        def keep_far(columns, value, k=k):
            far_out[k, :, columns] = (
                value.astype(F32) + pair_in[k, :, columns].astype(F32)
            ).astype(BF16)

        product(chips - 1 + k, keep_far)
        far_copy(k).start()

    def keep_sib(columns, value):
        sib_out[:, columns] = value

    product(tensors - 2, keep_sib)
    sib_copy().start()

    def keep_own(columns, value):
        total[:, columns] = value.astype(F32)

    product(tensors - 1, keep_own)

    def stage_copy(j, half, slot):
        return pltpu.make_async_copy(
            down_ref.at[2 * j + half], stage.at[slot, half], stage_sem.at[slot, half]
        )

    pairs = per_adapter // 2
    for half in range(2):
        stage_copy(0, half, 0).start()

    def lay(j, carry):
        slot = lax.rem(j, 2)

        @pl.when(j + 1 < pairs)
        def _():
            for half in range(2):
                stage_copy(j + 1, half, 1 - slot).start()

        for half in range(2):
            stage_copy(j, half, slot).wait()
        down[:, pl.ds(pl.multiple_of(j * 2 * rank_extent, 2 * rank_extent), 2 * rank_extent)] = (
            jnp.concatenate([stage[slot, 0], stage[slot, 1]], axis=1)
        )
        return carry

    lax.fori_loop(0, pairs, lay, 0)

    for copy in locals_:
        copy.wait()
    for d in range(1, owners):
        ids_copy(d, source(d)).wait_recv()

    lanes = 2 * rank_extent
    pick = (
        lax.broadcasted_iota(jnp.int32, (wide, lanes), 0) % rank_extent
        == lax.broadcasted_iota(jnp.int32, (wide, lanes), 1)
    ).astype(F32).astype(BF16)
    eye = lax.broadcasted_iota(jnp.int32, (slots, slots), 0) == lax.broadcasted_iota(
        jnp.int32, (slots, slots), 1
    )
    block_of = lax.broadcasted_iota(jnp.int32, (slots, wide), 1) // rank_extent

    def mask_of(c, s):
        numbers = ids_in[s, 0:1, c * slots : (c + 1) * slots]
        column = jnp.sum(jnp.where(eye, numbers.astype(F32), 0.0), axis=1, keepdims=True)
        return column.astype(jnp.int32) == block_of

    def rank_copy(c, d):
        to = lax.rem(t + d, tensors)
        return remote(
            rank_out.at[c],
            rank_in.at[c, d - 1],
            rank_send.at[c, d - 1],
            rank_recv.at[c, d - 1],
            "tensor",
            to,
        )

    def reduce_chunk(c):
        for d in range(1, owners):
            rows_copy(c, d, source(d)).wait_recv()
        full = jnp.dot(
            arrived[c].reshape(block, features), down[...], preferred_element_type=F32
        )
        for s in range(owners):
            mine = slice(s * slots, (s + 1) * slots)
            held = jnp.where(mask_of(c, s), full[mine], 0.0).astype(BF16)
            rank_out[c, mine] = jnp.dot(held, pick, preferred_element_type=F32).astype(BF16)
        for d in range(1, tensors):
            rank_copy(c, d).start()

    def lift_chunk(c):
        for d in range(1, tensors):
            rank_copy(c, d).wait_recv()
        reduced = rank_out[c].astype(F32)
        for d in range(1, tensors):
            reduced = reduced + rank_in[c, d - 1].astype(F32)
        spread = lax.dot_general(
            reduced.astype(BF16), pick, (((1,), (1,)), ((), ())), preferred_element_type=F32
        )
        held = jnp.concatenate(
            [
                jnp.where(mask_of(c, s), spread[s * slots : (s + 1) * slots], 0.0).astype(BF16)
                for s in range(owners)
            ],
            axis=0,
        )
        lifted[c] = (
            jnp.dot(held, up[...], preferred_element_type=F32)
            .astype(BF16)
            .reshape(owners, slots, features)
        )
        for d in range(1, owners):
            back_copy(c, d, me).start()
        back[c, me] = lifted[c, me]

    for c in range(CHUNKS):
        reduce_chunk(c)
        lift_chunk(c)

    sib_copy().wait_recv()
    total[...] += sib_in[...].astype(F32)
    for k in range(chips - 1):
        far_copy(k).wait_recv()
        total[...] += far_in[k].astype(F32)

    for c in range(CHUNKS):
        for d in range(1, owners):
            back_copy(c, d, source(d)).wait_recv()
        sum_ = total[...] + jnp.dot(
            place_ref[c], back[c].reshape(block, features), preferred_element_type=F32
        )
        if c + 1 < CHUNKS:
            total[...] = sum_
        else:
            out_ref[...] = sum_.astype(BF16)

    for d in range(1, owners):
        ids_copy(d, me).wait_send()
        for c in range(CHUNKS):
            rows_copy(c, d, me).wait_send()
            back_copy(c, d, me).wait_send()
    for k in range(chips - 1):
        pair_copy(k).wait_send()
        far_copy(k).wait_send()
    sib_copy().wait_send()
    for c in range(CHUNKS):
        for d in range(1, tensors):
            rank_copy(c, d).wait_send()


def on_device(context, output_weight, adapter_down, adapter_up, token_adapter):
    owners = lax.axis_size("owner")
    tensors = lax.axis_size("tensor")
    tokens, features = context.shape
    per_adapter, _, rank_extent = adapter_down.shape
    slots = tokens // 2 // CHUNKS
    wide = per_adapter * rank_extent
    tile = min(512, features)
    chips = tensors // CORES

    target = token_adapter // per_adapter
    within = token_adapter % per_adapter
    onehot = (target[:, None] == jnp.arange(owners)[None, :]).astype(BF16)
    before = (jnp.arange(tokens)[:, None] > jnp.arange(tokens)[None, :]).astype(BF16)
    counts = jnp.dot(before, onehot, preferred_element_type=F32)
    rank = jnp.sum(counts * onehot.astype(F32), axis=1).astype(jnp.int32)
    slot = (rank // slots * owners + target) * slots + rank % slots
    hit = slot[:, None] == jnp.arange(CHUNKS * owners * slots)[None, :]
    place = hit.astype(BF16)
    outgoing = (
        lax.dot_general(place, context, (((0,), (0,)), ((), ())), preferred_element_type=F32)
        .astype(BF16)
        .reshape(CHUNKS, owners, slots, features)
    )
    ids = jnp.max(jnp.where(hit, within[:, None], -1), axis=0).reshape(CHUNKS, owners, slots)
    ids = ids.transpose(1, 0, 2).reshape(owners, 1, CHUNKS * slots)
    ids = jnp.broadcast_to(ids, (owners, 8, CHUNKS * slots))
    place = place.reshape(tokens, CHUNKS, owners * slots).transpose(1, 0, 2)

    anywhere = pl.BlockSpec(memory_space=pl.ANY)
    vmem = pl.BlockSpec(memory_space=pltpu.VMEM)
    dma = pltpu.SemaphoreType.DMA
    return pl.pallas_call(
        functools.partial(kernel, owners, tensors, tile),
        out_shape=jax.ShapeDtypeStruct((tokens, features), BF16),
        in_specs=[vmem, anywhere, anywhere, anywhere, anywhere, anywhere, vmem],
        out_specs=vmem,
        scratch_shapes=[
            pltpu.VMEM((CHUNKS, owners, slots, features), BF16),
            pltpu.VMEM((owners, 8, CHUNKS * slots), jnp.int32),
            pltpu.VMEM((2, 2, features, rank_extent), BF16),
            pltpu.VMEM((features, wide), BF16),
            pltpu.VMEM((wide, features), BF16),
            pltpu.VMEM((2, features, tile), BF16),
            pltpu.VMEM((chips - 1, tokens, features), BF16),
            pltpu.VMEM((chips - 1, tokens, features), BF16),
            pltpu.VMEM((chips - 1, tokens, features), BF16),
            pltpu.VMEM((chips - 1, tokens, features), BF16),
            pltpu.VMEM((tokens, features), BF16),
            pltpu.VMEM((tokens, features), BF16),
            pltpu.VMEM((tokens, features), F32),
            pltpu.VMEM((CHUNKS, owners * slots, 2 * rank_extent), BF16),
            pltpu.VMEM((CHUNKS, tensors - 1, owners * slots, 2 * rank_extent), BF16),
            pltpu.VMEM((CHUNKS, owners, slots, features), BF16),
            pltpu.VMEM((CHUNKS, owners, slots, features), BF16),
            dma((2,)),
            dma((2, 2)),
            dma((2 + CHUNKS,)),
            dma((owners - 1,)),
            dma((owners - 1,)),
            dma((CHUNKS, owners - 1)),
            dma((CHUNKS, owners - 1)),
            dma((chips - 1,)),
            dma((chips - 1,)),
            dma((chips - 1,)),
            dma((chips - 1,)),
            dma,
            dma,
            dma((CHUNKS, tensors - 1)),
            dma((CHUNKS, tensors - 1)),
            dma((CHUNKS, owners - 1)),
            dma((CHUNKS, owners - 1)),
        ],
        compiler_params=pltpu.CompilerParams(
            collective_id=0, has_side_effects=True, vmem_limit_bytes=60 * 1024 * 1024
        ),
        cost_estimate=pl.CostEstimate(
            flops=2 * tokens * features * features * tensors,
            bytes_accessed=2 * features * features * tensors,
            transcendentals=0,
        ),
    )(
        context,
        output_weight,
        adapter_down,
        adapter_up.reshape(wide, features),
        outgoing,
        ids,
        place,
    )


def solution(mesh):
    placed = (
        P(("replica", "owner"), "tensor"),
        P("tensor", None),
        P("owner", "tensor", None),
        P("owner", None, "tensor"),
        P(("replica", "owner")),
    )
    return jax.shard_map(
        on_device,
        mesh=mesh,
        in_specs=placed,
        out_specs=P(("replica", "owner"), "tensor"),
        check_vma=False,
    )
```

time: 333 us -> 211 us (0.63); the launches traced: 328 us -> 211 us
  waiting for transfers between devices: 158 us -> 0 us
  Pallas kernels: 39.5 us -> 190 us
  local copies, waits for them, and re-layouts: 51.6 us -> 12.1 us
  other arithmetic: 23.3 us -> 2.29 us
  matrix products: 25.5 us -> 6.28 us
  starting transfers between devices: 16.2 us -> 0 us
  between operations: 13.5 us -> 0.03 us
    pallas_call x0 -> x1, Pallas kernels: none -> 190 us  [on_device(): pl.pallas_call(functools.partial(kernel, owners, tensors, tile), out_shap...]
    all_to_all x3 -> x0, waiting for transfers between devices: 154 us -> none  [the longest x1 89.3 us: on_device(): lax.all_to_all(lifted.reshape(owners, capacity, feature_columns), 'owner'...]
    another operation x2 -> x0, Pallas kernels: 37.6 us -> none
    dot_general x1 -> x2, matrix products: 25.5 us -> 6.28 us  [the longest x1 6.02 us: on_device(): lax.dot_general(place, context, (((0,), (0,)), ((), ())), preferred_eleme...]
    gather x2 -> x0, local copies, waits for them, and re-layouts: 18.7 us -> none  [the longest x1 11.6 us: on_device(): sorted_rows = arrived[ordering]]
    all_to_all x3 -> x0, starting transfers between devices: 16 us -> none  [the longest x1 5.6 us: on_device(): lax.all_to_all(lifted.reshape(owners, capacity, feature_columns), 'owner'...]
    concatenate x2 -> x0, local copies, waits for them, and re-layouts: 14 us -> none  [the longest x1 9.15 us: on_device(): jnp.concatenate([adapter_down, jnp.zeros((1, feature_columns, rank_extent...]
    scatter x1 -> x0, other arithmetic: 10.6 us -> none  [on_device(): lifted = jnp.zeros_like(lifted_sorted).at[ordering].set(lifted_sorted)]
  transfers between devices with their start and end apart: 5 -> 0, of which waited for: 3 -> 0; matrix products, arithmetic and copies ran while one was open for 24% -> 0% of each run, Pallas kernels for 6% -> 0%
where the time goes in v2:
time: 211 us
  Pallas kernels  190 us (90%)
  local copies, waits for them, and re-layouts  12.1 us (6%)
  matrix products  6.28 us (3%)
  other arithmetic  2.29 us (1%)
    pallas_call x1, Pallas kernels, on_device(): pl.pallas_call(functools.partial(kernel, owners, tensors, tile), out_shap...  190 us
    unnamed x2, local copies, waits for them, and re-layouts  11.5 us
    dot_general x1, matrix products, on_device(): lax.dot_general(place, context, (((0,), (0,)), ((), ())), preferred_eleme...  6.02 us

profile of v2, /device:TPU:8, one launch (start us, length us, event | category | flops | bytes accessed | tf_op | source)
XLA Modules:
  0.0 210.6 jit_solution(16766824722044457726)
XLA Ops:
  0.0 0.7 add_select_fusion
  0.7 0.3 fusion
  1.0 0.4 select_reduce_fusion
  1.4 0.6 broadcast_in_dim.29.ids_out_ref
  2.0 1.2 compare_convert_fusion.place_ref
  3.2 6.0 %convolution_convert_fusion = bf16[1024,2048]{1,0:T(8,128)(2,1)} fusion(bf16[512,2048]{1,0:T(8,128)(2,1)} %ctx_ref.1, s32[512]{0:T(512)S(1)} %fusion.7), kind=kOutput, calls=%fused_computation | convolution fusion | flops 2150105088 | bytes 6293504 | tf_op jit(solution)/shard_map/dot_general | solution.py:370
  9.2 8.4 %copy.8.down_ref = bf16[16,2048,64]{2,1,0:T(8,128)(2,1)} copy(bf16[16,2048,64]{1,2,0:T(8,128)(2,1)} %param.7) | data formatting | bytes 8388608 | tf_op args[2]
  17.6 189.9 %shard_map.55 = bf16[512,2048]{1,0:T(8,128)(2,1)} custom-call(bf16[512,2048]{1,0:T(8,128)(2,1)} %ctx_ref.1, bf16[2048,8192]{1,0:T(8,128)(2,1)} %w_ref.1, bf16[16,2048,64]{2,1,0:T(8,128)(2,1)} %copy.8.down_ref, bf16[1024,2048]{1,0:T(8,128)(2,1)} %bitcast.9, bf16[2,4,128,2048]{3,2,1,0:T(8,128)(2,1)} %bitcast.10, s32[4,8,256]{2,1,0:T(8,128)} %broadcast_in_dim.29.ids_out_ref, ...), custom_call_target="tpu_custom_call" | custom-call | flops 17179869184 | bytes 33554432 | tf_op jit(solution)/shard_map/pallas_call | solution.py:382
  207.4 3.2 %copy.10 = bf16[512,2048]{1,0:T(8,128)(2,1)} copy(bf16[512,2048]{1,0:T(8,128)(2,1)} %shard_map.55) | data formatting | bytes 4194304
  (2 shorter events, 0.0 us)

commit v3 on v2

--- a/solution.py
+++ b/solution.py
@@ -29,17 +29,17 @@
     owners,
     tensors,
     tile,
+    rank_extent,
     ctx_ref,
     w_ref,
     down_ref,
     up_ref,
-    outgoing_ref,
     ids_out_ref,
     place_ref,
     out_ref,
+    outgoing,
     arrived,
     ids_in,
-    stage,
     down,
     up,
     wbuf,
@@ -55,7 +55,6 @@
     lifted,
     back,
     w_sem,
-    stage_sem,
     local_sem,
     ids_send,
     ids_recv,
@@ -78,9 +77,8 @@
     chips = tensors // CORES
     sibling = y * CORES + 1 - core
     rows, features = ctx_ref.shape
-    per_adapter, _, rank_extent = down_ref.shape
-    wide = per_adapter * rank_extent
-    slots = outgoing_ref.shape[2]
+    wide = down_ref.shape[0]
+    slots = place_ref.shape[2] // owners
     block = owners * slots
 
     barrier = pltpu.get_barrier_semaphore()
@@ -103,7 +101,7 @@
     def rows_copy(c, d, at):
         to = lax.rem(me + d, owners)
         return remote(
-            outgoing_ref.at[c, to],
+            outgoing.at[c, to],
             arrived.at[c, at],
             out_send.at[c, d - 1],
             out_recv.at[c, d - 1],
@@ -122,18 +120,29 @@
 
     for d in range(1, owners):
         ids_copy(d, me).start()
+
+    def chosen(c, to):
+        columns = pl.ds(pl.multiple_of(to * slots, slots), slots)
+        return lax.dot_general(
+            place_ref[c, :, columns],
+            ctx_ref[...],
+            (((0,), (0,)), ((), ())),
+            preferred_element_type=F32,
+        ).astype(BF16)
+
     for c in range(CHUNKS):
         for d in range(1, owners):
+            to = lax.rem(me + d, owners)
+            outgoing[c, to] = chosen(c, to)
             rows_copy(c, d, me).start()
 
     locals_ = [pltpu.make_async_copy(up_ref, up, local_sem.at[0])]
     locals_.append(pltpu.make_async_copy(ids_out_ref.at[me], ids_in.at[me], local_sem.at[1]))
-    for c in range(CHUNKS):
-        locals_.append(
-            pltpu.make_async_copy(outgoing_ref.at[c, me], arrived.at[c, me], local_sem.at[2 + c])
-        )
+    locals_.append(pltpu.make_async_copy(down_ref, down, local_sem.at[2]))
     for copy in locals_:
         copy.start()
+    for c in range(CHUNKS):
+        arrived[c, me] = chosen(c, me)
 
     steps = features // tile
     others = [lax.rem(y + 1 + k, chips) for k in range(chips - 1)]
@@ -216,32 +225,6 @@
         total[:, columns] = value.astype(F32)
 
     product(tensors - 1, keep_own)
-
-    def stage_copy(j, half, slot):
-        return pltpu.make_async_copy(
-            down_ref.at[2 * j + half], stage.at[slot, half], stage_sem.at[slot, half]
-        )
-
-    pairs = per_adapter // 2
-    for half in range(2):
-        stage_copy(0, half, 0).start()
-
-    def lay(j, carry):
-        slot = lax.rem(j, 2)
-
-        @pl.when(j + 1 < pairs)
-        def _():
-            for half in range(2):
-                stage_copy(j + 1, half, 1 - slot).start()
-
-        for half in range(2):
-            stage_copy(j, half, slot).wait()
-        down[:, pl.ds(pl.multiple_of(j * 2 * rank_extent, 2 * rank_extent), 2 * rank_extent)] = (
-            jnp.concatenate([stage[slot, 0], stage[slot, 1]], axis=1)
-        )
-        return carry
-
-    lax.fori_loop(0, pairs, lay, 0)
 
     for copy in locals_:
         copy.wait()
@@ -277,8 +260,11 @@
     def reduce_chunk(c):
         for d in range(1, owners):
             rows_copy(c, d, source(d)).wait_recv()
-        full = jnp.dot(
-            arrived[c].reshape(block, features), down[...], preferred_element_type=F32
+        full = lax.dot_general(
+            arrived[c].reshape(block, features),
+            down[...],
+            (((1,), (1,)), ((), ())),
+            preferred_element_type=F32,
         )
         for s in range(owners):
             mine = slice(s * slots, (s + 1) * slots)
@@ -366,11 +352,6 @@
     slot = (rank // slots * owners + target) * slots + rank % slots
     hit = slot[:, None] == jnp.arange(CHUNKS * owners * slots)[None, :]
     place = hit.astype(BF16)
-    outgoing = (
-        lax.dot_general(place, context, (((0,), (0,)), ((), ())), preferred_element_type=F32)
-        .astype(BF16)
-        .reshape(CHUNKS, owners, slots, features)
-    )
     ids = jnp.max(jnp.where(hit, within[:, None], -1), axis=0).reshape(CHUNKS, owners, slots)
     ids = ids.transpose(1, 0, 2).reshape(owners, 1, CHUNKS * slots)
     ids = jnp.broadcast_to(ids, (owners, 8, CHUNKS * slots))
@@ -380,15 +361,15 @@
     vmem = pl.BlockSpec(memory_space=pltpu.VMEM)
     dma = pltpu.SemaphoreType.DMA
     return pl.pallas_call(
-        functools.partial(kernel, owners, tensors, tile),
+        functools.partial(kernel, owners, tensors, tile, rank_extent),
         out_shape=jax.ShapeDtypeStruct((tokens, features), BF16),
-        in_specs=[vmem, anywhere, anywhere, anywhere, anywhere, anywhere, vmem],
+        in_specs=[vmem, anywhere, anywhere, anywhere, anywhere, vmem],
         out_specs=vmem,
         scratch_shapes=[
             pltpu.VMEM((CHUNKS, owners, slots, features), BF16),
+            pltpu.VMEM((CHUNKS, owners, slots, features), BF16),
             pltpu.VMEM((owners, 8, CHUNKS * slots), jnp.int32),
-            pltpu.VMEM((2, 2, features, rank_extent), BF16),
-            pltpu.VMEM((features, wide), BF16),
+            pltpu.VMEM((wide, features), BF16),
             pltpu.VMEM((wide, features), BF16),
             pltpu.VMEM((2, features, tile), BF16),
             pltpu.VMEM((chips - 1, tokens, features), BF16),
@@ -403,8 +384,7 @@
             pltpu.VMEM((CHUNKS, owners, slots, features), BF16),
             pltpu.VMEM((CHUNKS, owners, slots, features), BF16),
             dma((2,)),
-            dma((2, 2)),
-            dma((2 + CHUNKS,)),
+            dma((3,)),
             dma((owners - 1,)),
             dma((owners - 1,)),
             dma((CHUNKS, owners - 1)),
@@ -431,9 +411,8 @@
     )(
         context,
         output_weight,
-        adapter_down,
+        adapter_down.transpose(0, 2, 1).reshape(wide, features),
         adapter_up.reshape(wide, features),
-        outgoing,
         ids,
         place,
     )

time: 211 us -> 197 us (0.934)
  local copies, waits for them, and re-layouts: 12.1 us -> 3.76 us
  matrix products: 6.28 us -> 0.26 us
    unnamed x2 -> x1, local copies, waits for them, and re-layouts: 11.5 us -> 3.16 us
    dot_general x1 -> x0, matrix products: 6.02 us -> none  [on_device(): lax.dot_general(place, context, (((0,), (0,)), ((), ())), preferred_eleme...]
where the time goes in v3:
time: 197 us
  Pallas kernels  190 us (96%)
  local copies, waits for them, and re-layouts  3.76 us (2%)
  other arithmetic  2.29 us (1%)
    pallas_call x1, Pallas kernels, on_device(): pl.pallas_call(functools.partial(kernel, owners, tensors, tile, rank_exte...  190 us

profile of v3, /device:TPU:8, one launch (start us, length us, event | category | flops | bytes accessed | tf_op | source)
XLA Modules:
  0.0 196.6 jit_solution(9611806960876278314)
XLA Ops:
  0.0 0.7 add_select_fusion.3
  0.7 0.3 fusion
  1.0 0.4 select_reduce_fusion
  1.4 0.6 broadcast_in_dim.29.ids_out_ref
  2.0 1.2 compare_convert_fusion.place_ref
  3.2 190.2 %shard_map.55 = bf16[512,2048]{1,0:T(8,128)(2,1)} custom-call(bf16[512,2048]{1,0:T(8,128)(2,1)} %ctx_ref.1, bf16[2048,8192]{1,0:T(8,128)(2,1)} %w_ref.1, bf16[1024,2048]{1,0:T(8,128)(2,1)} %bitcast.10, bf16[1024,2048]{1,0:T(8,128)(2,1)} %bitcast.11, s32[4,8,256]{2,1,0:T(8,128)} %broadcast_in_dim.29.ids_out_ref, ...), custom_call_target="tpu_custom_call" | custom-call | flops 17179869184 | bytes 33554432 | tf_op jit(solution)/shard_map/pallas_call | solution.py:363
  193.4 3.2 %copy.7 = bf16[512,2048]{1,0:T(8,128)(2,1)} copy(bf16[512,2048]{1,0:T(8,128)(2,1)} %shard_map.55) | data formatting | bytes 4194304
  (2 shorter events, 0.0 us)

commit v4 on v3

--- a/solution.py
+++ b/solution.py
@@ -333,9 +333,442 @@
             rank_copy(c, d).wait_send()
 
 
+def fast_kernel(
+    owners,
+    tensors,
+    tile,
+    rank_extent,
+    ctx_ref,
+    w_ref,
+    down_ref,
+    up_ref,
+    ids_out_ref,
+    place_ref,
+    extra_ref,
+    out_ref,
+    flag_ref,
+    outgoing,
+    arrived,
+    ids_in,
+    down,
+    up,
+    wbuf,
+    pair_out,
+    pair_in,
+    far_out,
+    far_in,
+    sib_out,
+    sib_in,
+    total,
+    rank_out,
+    rank_in,
+    lifted,
+    back,
+    w_sem,
+    local_sem,
+    ids_send,
+    ids_recv,
+    out_send,
+    out_recv,
+    pair_send,
+    pair_recv,
+    far_send,
+    far_recv,
+    sib_send,
+    sib_recv,
+    rank_send,
+    rank_recv,
+    back_send,
+    back_recv,
+    sums_in,
+    flags,
+    extra_send,
+    extra_recv,
+    sums_send,
+    sums_recv,
+    flag_send,
+    flag_recv,
+):
+    me = lax.axis_index("owner")
+    t = lax.axis_index("tensor")
+    y, core = t // CORES, t % CORES
+    chips = tensors // CORES
+    sibling = y * CORES + 1 - core
+    rows, features = ctx_ref.shape
+    wide = down_ref.shape[0]
+    slots = place_ref.shape[2] // owners
+    block = owners * slots
+
+    barrier = pltpu.get_barrier_semaphore()
+    for d in range(1, owners):
+        pl.semaphore_signal(
+            barrier, inc=1, device_id={"owner": lax.rem(me + d, owners)}, device_id_type=MESH
+        )
+    for d in range(1, tensors):
+        pl.semaphore_signal(
+            barrier, inc=1, device_id={"tensor": lax.rem(t + d, tensors)}, device_id_type=MESH
+        )
+    replicas = flags.shape[0]
+    part = lax.axis_index("replica")
+    for d in range(1, replicas):
+        pl.semaphore_signal(
+            barrier,
+            inc=1,
+            device_id={"replica": lax.rem(part + d, replicas)},
+            device_id_type=MESH,
+        )
+    pl.semaphore_wait(barrier, owners + tensors + replicas - 3)
+
+    def ids_copy(d, at):
+        to = lax.rem(me + d, owners)
+        return remote(
+            ids_out_ref.at[to], ids_in.at[at], ids_send.at[d - 1], ids_recv.at[d - 1], "owner", to
+        )
+
+    def rows_copy(c, d, at):
+        to = lax.rem(me + d, owners)
+        return remote(
+            outgoing.at[c, to],
+            arrived.at[c, at],
+            out_send.at[c, d - 1],
+            out_recv.at[c, d - 1],
+            "owner",
+            to,
+        )
+
+    def back_copy(c, d, at):
+        to = lax.rem(me + d, owners)
+        return remote(
+            lifted.at[c, to], back.at[c, at], back_send.at[c, d - 1], back_recv.at[c, d - 1], "owner", to
+        )
+
+    def source(d):
+        return lax.rem(me - d + owners, owners)
+
+    for d in range(1, owners):
+        ids_copy(d, me).start()
+
+    def chosen(c, to):
+        columns = pl.ds(pl.multiple_of(to * slots, slots), slots)
+        return lax.dot_general(
+            place_ref[c, :, columns],
+            ctx_ref[...],
+            (((0,), (0,)), ((), ())),
+            preferred_element_type=F32,
+        ).astype(BF16)
+
+    def extra_copy(way, s):
+        return remote(
+            arrived.at[1, s],
+            arrived.at[1, s],
+            extra_send.at[way, s],
+            extra_recv.at[s],
+            "owner",
+            lax.rem(me + (1 if way else owners - 1), owners),
+        )
+
+    def pass_on(s, way):
+        @pl.when((me + 1 < owners) if way else (me > 0))
+        def _():
+            extra_copy(way, s).start()
+
+    arrived[1, me] = lax.dot_general(
+        extra_ref[...], ctx_ref[...], (((0,), (0,)), ((), ())), preferred_element_type=F32
+    ).astype(BF16)
+    pass_on(me, 1)
+    pass_on(me, 0)
+
+    for d in range(1, owners):
+        to = lax.rem(me + d, owners)
+        outgoing[0, to] = chosen(0, to)
+        rows_copy(0, d, me).start()
+
+    locals_ = [pltpu.make_async_copy(up_ref, up, local_sem.at[0])]
+    locals_.append(pltpu.make_async_copy(ids_out_ref.at[me], ids_in.at[me], local_sem.at[1]))
+    locals_.append(pltpu.make_async_copy(down_ref, down, local_sem.at[2]))
+    for copy in locals_:
+        copy.start()
+    arrived[0, me] = chosen(0, me)
+
+    steps = features // tile
+    others = [lax.rem(y + 1 + k, chips) for k in range(chips - 1)]
+    order = [o * CORES + 1 - core for o in others]
+    order += [o * CORES + core for o in others]
+    order += [sibling, t]
+
+    def fetch(column, slot):
+        return pltpu.make_async_copy(
+            w_ref.at[:, pl.ds(pl.multiple_of(column, tile), tile)], wbuf.at[slot], w_sem.at[slot]
+        )
+
+    def product(p, store):
+        first = order[p] * features
+        after = order[p + 1] * features if p + 1 < tensors else None
+
+        def body(j, carry):
+            slot = lax.rem(p * steps + j, 2)
+            if after is not None:
+                fetch(jnp.where(j + 1 < steps, first + (j + 1) * tile, after), 1 - slot).start()
+            else:
+
+                @pl.when(j + 1 < steps)
+                def _():
+                    fetch(first + (j + 1) * tile, 1 - slot).start()
+
+            fetch(first + j * tile, slot).wait()
+            store(
+                pl.ds(pl.multiple_of(j * tile, tile), tile),
+                jnp.dot(ctx_ref[...], wbuf[slot], preferred_element_type=F32).astype(BF16),
+            )
+            return carry
+
+        lax.fori_loop(0, steps, body, 0)
+
+    def pair_copy(k):
+        return remote(
+            pair_out.at[k], pair_in.at[k], pair_send.at[k], pair_recv.at[k], "tensor", sibling
+        )
+
+    def far_copy(k):
+        return remote(
+            far_out.at[k],
+            far_in.at[k],
+            far_send.at[k],
+            far_recv.at[k],
+            "tensor",
+            others[k] * CORES + core,
+        )
+
+    def sib_copy():
+        return remote(sib_out, sib_in, sib_send, sib_recv, "tensor", sibling)
+
+    fetch(order[0] * features, 0).start()
+    for k in range(chips - 1):
+
+        def keep_pair(columns, value, k=k):
+            pair_out[k, :, columns] = value
+
+        product(k, keep_pair)
+        pair_copy(k).start()
+    for k in range(chips - 1):
+        pair_copy(k).wait_recv()
+
+        def keep_far(columns, value, k=k):
+            far_out[k, :, columns] = (
+                value.astype(F32) + pair_in[k, :, columns].astype(F32)
+            ).astype(BF16)
+
+        product(chips - 1 + k, keep_far)
+        far_copy(k).start()
+
+    def keep_sib(columns, value):
+        sib_out[:, columns] = value
+
+    product(tensors - 2, keep_sib)
+    sib_copy().start()
+
+    def keep_own(columns, value):
+        total[:, columns] = value.astype(F32)
+
+    product(tensors - 1, keep_own)
+
+    for copy in locals_:
+        copy.wait()
+    for d in range(1, owners):
+        ids_copy(d, source(d)).wait_recv()
+
+    lanes = 2 * rank_extent
+    pick = (
+        lax.broadcasted_iota(jnp.int32, (wide, lanes), 0) % rank_extent
+        == lax.broadcasted_iota(jnp.int32, (wide, lanes), 1)
+    ).astype(F32).astype(BF16)
+    eye = lax.broadcasted_iota(jnp.int32, (slots, slots), 0) == lax.broadcasted_iota(
+        jnp.int32, (slots, slots), 1
+    )
+    block_of = lax.broadcasted_iota(jnp.int32, (slots, wide), 1) // rank_extent
+
+    def mask_of(c, s):
+        numbers = ids_in[s, 0:1, c * slots : (c + 1) * slots]
+        column = jnp.sum(jnp.where(eye, numbers.astype(F32), 0.0), axis=1, keepdims=True)
+        return column.astype(jnp.int32) == block_of
+
+    def rank_copy(c, d):
+        to = lax.rem(t + d, tensors)
+        return remote(
+            rank_out.at[c],
+            rank_in.at[c, d - 1],
+            rank_send.at[c, d - 1],
+            rank_recv.at[c, d - 1],
+            "tensor",
+            to,
+        )
+
+    def reduce_chunk(c):
+        if c == 0:
+            for d in range(1, owners):
+                rows_copy(c, d, source(d)).wait_recv()
+        full = lax.dot_general(
+            arrived[c].reshape(block, features),
+            down[...],
+            (((1,), (1,)), ((), ())),
+            preferred_element_type=F32,
+        )
+        for s in range(owners):
+            mine = slice(s * slots, (s + 1) * slots)
+            held = jnp.where(mask_of(c, s), full[mine], 0.0).astype(BF16)
+            rank_out[c, mine] = jnp.dot(held, pick, preferred_element_type=F32).astype(BF16)
+        for d in range(1, tensors):
+            rank_copy(c, d).start()
+
+    def lift_chunk(c):
+        for d in range(1, tensors):
+            rank_copy(c, d).wait_recv()
+        reduced = rank_out[c].astype(F32)
+        for d in range(1, tensors):
+            reduced = reduced + rank_in[c, d - 1].astype(F32)
+        spread = lax.dot_general(
+            reduced.astype(BF16), pick, (((1,), (1,)), ((), ())), preferred_element_type=F32
+        )
+        held = jnp.concatenate(
+            [
+                jnp.where(mask_of(c, s), spread[s * slots : (s + 1) * slots], 0.0).astype(BF16)
+                for s in range(owners)
+            ],
+            axis=0,
+        )
+        lifted[c] = (
+            jnp.dot(held, up[...], preferred_element_type=F32)
+            .astype(BF16)
+            .reshape(owners, slots, features)
+        )
+        if c == 0:
+            for d in range(1, owners):
+                back_copy(c, d, me).start()
+            back[c, me] = lifted[c, me]
+
+    flag = ids_in[0]
+    for s in range(1, owners):
+        flag = jnp.maximum(flag, ids_in[s])
+    flags[0] = flag
+
+    def flag_copy(d):
+        return remote(
+            flags.at[0],
+            flags.at[d],
+            flag_send.at[d - 1],
+            flag_recv.at[d - 1],
+            "replica",
+            lax.rem(part + d, replicas),
+        )
+
+    for d in range(1, replicas):
+        flag_copy(d).start()
+
+    for k in range(1, owners):
+        for way in range(2):
+            s = me - k if way else me + k
+
+            @pl.when((s >= 0) if way else (s < owners))
+            def _(s=s, way=way):
+                extra_copy(way, s).wait_recv()
+                pass_on(s, way)
+
+    def sums_copy(way, s):
+        return remote(
+            lifted.at[1, s],
+            sums_in.at[way, s],
+            sums_send.at[way, s],
+            sums_recv.at[way, s],
+            "owner",
+            lax.rem(me + (1 if way else owners - 1), owners),
+        )
+
+    def add_sum(way, s):
+        @pl.when((me > 0) if way else (me + 1 < owners))
+        def _():
+            sums_copy(way, s).wait_recv()
+            lifted[1, s] = lifted[1, s] + sums_in[way, s]
+
+    reduce_chunk(1)
+    lift_chunk(1)
+
+    @pl.when(me == 0)
+    def _():
+        for s in range(owners - 1, 0, -1):
+            sums_copy(1, s).start()
+
+    @pl.when(me == owners - 1)
+    def _():
+        for s in range(owners - 1):
+            sums_copy(0, s).start()
+
+    reduce_chunk(0)
+    lift_chunk(0)
+
+    for k in range(owners - 1, 0, -1):
+        for way in range(2):
+            s = me + k if way else me - k
+            inside = (s < owners) & (me > 0) if way else (s >= 0) & (me + 1 < owners)
+
+            @pl.when(inside)
+            def _(s=s, way=way):
+                sums_copy(way, s).wait_recv()
+                lifted[1, s] = lifted[1, s] + sums_in[way, s]
+                sums_copy(way, s).start()
+
+    sib_copy().wait_recv()
+    total[...] += sib_in[...].astype(F32)
+    for k in range(chips - 1):
+        far_copy(k).wait_recv()
+        total[...] += far_in[k].astype(F32)
+
+    for d in range(1, owners):
+        back_copy(0, d, source(d)).wait_recv()
+    total[...] += jnp.dot(
+        place_ref[0], back[0].reshape(block, features), preferred_element_type=F32
+    )
+    add_sum(0, me)
+    add_sum(1, me)
+    out_ref[...] = (
+        total[...] + jnp.dot(extra_ref[...], lifted[1, me], preferred_element_type=F32)
+    ).astype(BF16)
+
+    for d in range(1, replicas):
+        flag_copy(d).wait_recv()
+    flag = flags[0]
+    for d in range(1, replicas):
+        flag = jnp.maximum(flag, flags[d])
+    flag_ref[...] = flag
+
+    for d in range(1, replicas):
+        flag_copy(d).wait_send()
+    for way in range(2):
+        for s in range(owners):
+
+            @pl.when(((s <= me) & (me + 1 < owners)) if way else ((s >= me) & (me > 0)))
+            def _(s=s, way=way):
+                extra_copy(way, s).wait_send()
+
+            @pl.when(((s > me) & (me + 1 < owners)) if way else ((s < me) & (me > 0)))
+            def _(s=s, way=way):
+                sums_copy(way, s).wait_send()
+    for d in range(1, owners):
+        ids_copy(d, me).wait_send()
+        rows_copy(0, d, me).wait_send()
+        back_copy(0, d, me).wait_send()
+    for k in range(chips - 1):
+        pair_copy(k).wait_send()
+        far_copy(k).wait_send()
+    sib_copy().wait_send()
+    for c in range(CHUNKS):
+        for d in range(1, tensors):
+            rank_copy(c, d).wait_send()
+
+
 def on_device(context, output_weight, adapter_down, adapter_up, token_adapter):
     owners = lax.axis_size("owner")
     tensors = lax.axis_size("tensor")
+    replicas = lax.axis_size("replica")
     tokens, features = context.shape
     per_adapter, _, rank_extent = adapter_down.shape
     slots = tokens // 2 // CHUNKS
@@ -357,48 +790,80 @@
     ids = jnp.broadcast_to(ids, (owners, 8, CHUNKS * slots))
     place = place.reshape(tokens, CHUNKS, owners * slots).transpose(1, 0, 2)
 
+    late = rank >= slots
+    order = jnp.dot(before, late.astype(BF16)[:, None], preferred_element_type=F32)[:, 0]
+    listed = late[:, None] & (order.astype(jnp.int32)[:, None] == jnp.arange(slots)[None, :])
+    extra = listed.astype(BF16)
+    overflow = (jnp.sum(late.astype(jnp.int32)) > slots).astype(jnp.int32)
+    extra_ids = jnp.max(
+        jnp.where(
+            listed[None] & (target[None, :] == jnp.arange(owners)[:, None])[:, :, None],
+            within[None, :, None],
+            -1,
+        ),
+        axis=1,
+    )
+    fast_ids = jnp.concatenate([ids[:, 0, :slots], extra_ids], axis=1)[:, None, :]
+    fast_ids = jnp.concatenate(
+        [fast_ids, jnp.full((owners, 7, CHUNKS * slots), overflow, jnp.int32)], axis=1
+    )
+
     anywhere = pl.BlockSpec(memory_space=pl.ANY)
     vmem = pl.BlockSpec(memory_space=pltpu.VMEM)
     dma = pltpu.SemaphoreType.DMA
-    return pl.pallas_call(
-        functools.partial(kernel, owners, tensors, tile, rank_extent),
-        out_shape=jax.ShapeDtypeStruct((tokens, features), BF16),
-        in_specs=[vmem, anywhere, anywhere, anywhere, anywhere, vmem],
-        out_specs=vmem,
-        scratch_shapes=[
-            pltpu.VMEM((CHUNKS, owners, slots, features), BF16),
-            pltpu.VMEM((CHUNKS, owners, slots, features), BF16),
-            pltpu.VMEM((owners, 8, CHUNKS * slots), jnp.int32),
-            pltpu.VMEM((wide, features), BF16),
-            pltpu.VMEM((wide, features), BF16),
-            pltpu.VMEM((2, features, tile), BF16),
-            pltpu.VMEM((chips - 1, tokens, features), BF16),
-            pltpu.VMEM((chips - 1, tokens, features), BF16),
-            pltpu.VMEM((chips - 1, tokens, features), BF16),
-            pltpu.VMEM((chips - 1, tokens, features), BF16),
-            pltpu.VMEM((tokens, features), BF16),
-            pltpu.VMEM((tokens, features), BF16),
-            pltpu.VMEM((tokens, features), F32),
-            pltpu.VMEM((CHUNKS, owners * slots, 2 * rank_extent), BF16),
-            pltpu.VMEM((CHUNKS, tensors - 1, owners * slots, 2 * rank_extent), BF16),
-            pltpu.VMEM((CHUNKS, owners, slots, features), BF16),
-            pltpu.VMEM((CHUNKS, owners, slots, features), BF16),
-            dma((2,)),
-            dma((3,)),
-            dma((owners - 1,)),
-            dma((owners - 1,)),
-            dma((CHUNKS, owners - 1)),
-            dma((CHUNKS, owners - 1)),
-            dma((chips - 1,)),
-            dma((chips - 1,)),
-            dma((chips - 1,)),
-            dma((chips - 1,)),
-            dma,
-            dma,
-            dma((CHUNKS, tensors - 1)),
-            dma((CHUNKS, tensors - 1)),
-            dma((CHUNKS, owners - 1)),
-            dma((CHUNKS, owners - 1)),
+    scratch = lambda depth: [
+        pltpu.VMEM((depth, owners, slots, features), BF16),
+        pltpu.VMEM((CHUNKS, owners, slots, features), BF16),
+        pltpu.VMEM((owners, 8, CHUNKS * slots), jnp.int32),
+        pltpu.VMEM((wide, features), BF16),
+        pltpu.VMEM((wide, features), BF16),
+        pltpu.VMEM((2, features, tile), BF16),
+        pltpu.VMEM((chips - 1, tokens, features), BF16),
+        pltpu.VMEM((chips - 1, tokens, features), BF16),
+        pltpu.VMEM((chips - 1, tokens, features), BF16),
+        pltpu.VMEM((chips - 1, tokens, features), BF16),
+        pltpu.VMEM((tokens, features), BF16),
+        pltpu.VMEM((tokens, features), BF16),
+        pltpu.VMEM((tokens, features), F32),
+        pltpu.VMEM((CHUNKS, owners * slots, 2 * rank_extent), BF16),
+        pltpu.VMEM((CHUNKS, tensors - 1, owners * slots, 2 * rank_extent), BF16),
+        pltpu.VMEM((CHUNKS, owners, slots, features), BF16),
+        pltpu.VMEM((depth, owners, slots, features), BF16),
+        dma((2,)),
+        dma((3,)),
+        dma((owners - 1,)),
+        dma((owners - 1,)),
+        dma((CHUNKS, owners - 1)),
+        dma((CHUNKS, owners - 1)),
+        dma((chips - 1,)),
+        dma((chips - 1,)),
+        dma((chips - 1,)),
+        dma((chips - 1,)),
+        dma,
+        dma,
+        dma((CHUNKS, tensors - 1)),
+        dma((CHUNKS, tensors - 1)),
+        dma((CHUNKS, owners - 1)),
+        dma((CHUNKS, owners - 1)),
+    ]
+    projected, flag = pl.pallas_call(
+        functools.partial(fast_kernel, owners, tensors, tile, rank_extent),
+        out_shape=(
+            jax.ShapeDtypeStruct((tokens, features), BF16),
+            jax.ShapeDtypeStruct((8, CHUNKS * slots), jnp.int32),
+        ),
+        in_specs=[vmem, anywhere, anywhere, anywhere, anywhere, vmem, vmem],
+        out_specs=(vmem, vmem),
+        scratch_shapes=scratch(1)
+        + [
+            pltpu.VMEM((2, owners, slots, features), BF16),
+            pltpu.VMEM((replicas, 8, CHUNKS * slots), jnp.int32),
+            dma((2, owners)),
+            dma((owners,)),
+            dma((2, owners)),
+            dma((2, owners)),
+            dma((replicas - 1,)),
+            dma((replicas - 1,)),
         ],
         compiler_params=pltpu.CompilerParams(
             collective_id=0, has_side_effects=True, vmem_limit_bytes=60 * 1024 * 1024
@@ -413,8 +878,37 @@
         output_weight,
         adapter_down.transpose(0, 2, 1).reshape(wide, features),
         adapter_up.reshape(wide, features),
+        fast_ids,
+        place[:1],
+        extra,
+    )
+
+    def whole(ids, place):
+      return pl.pallas_call(
+        functools.partial(kernel, owners, tensors, tile, rank_extent),
+        out_shape=jax.ShapeDtypeStruct((tokens, features), BF16),
+        in_specs=[vmem, anywhere, anywhere, anywhere, anywhere, vmem],
+        out_specs=vmem,
+        scratch_shapes=scratch(CHUNKS),
+        compiler_params=pltpu.CompilerParams(
+            collective_id=1, has_side_effects=True, vmem_limit_bytes=60 * 1024 * 1024
+        ),
+        cost_estimate=pl.CostEstimate(
+            flops=2 * tokens * features * features * tensors,
+            bytes_accessed=2 * features * features * tensors,
+            transcendentals=0,
+        ),
+    )(
+        context,
+        output_weight,
+        adapter_down.transpose(0, 2, 1).reshape(wide, features),
+        adapter_up.reshape(wide, features),
         ids,
         place,
+    )
+
+    return lax.cond(
+        flag[1, 0] > 0, lambda: whole(ids, place), lambda: projected
     )
 
 

time: 197 us -> 184 us (0.934)
  the two profiles are of different devices: /device:TPU:8 before, /device:TPU:23 now
where the time goes in v4:
time: 184 us
  Pallas kernels  175 us (95%)
  local copies, waits for them, and re-layouts  3.96 us (2%)
  other arithmetic  3.33 us (2%)
    pallas_call x1, Pallas kernels, on_device(): pl.pallas_call(functools.partial(fast_kernel, owners, tensors, tile, rank...  175 us

profile of v4, /device:TPU:23, one launch (start us, length us, event | category | flops | bytes accessed | tf_op | source)
XLA Modules:
  0.0 183.7 jit_solution(6543448060375282569)
XLA Ops:
  0.0 0.7 add_select_fusion.3
  0.7 0.3 fusion
  1.0 0.6 convert_reduce_fusion
  2.3 0.2 fusion.1
  2.5 0.4 select_reduce_fusion
  2.9 0.8 fusion.12
  3.8 0.5 select_reduce_fusion.1
  4.3 0.6 concatenate.7.ids_out_ref
  4.9 0.2 compare_convert_fusion
  5.1 0.8 slice.14.place_ref
  6.0 174.5 %shard_map.57 = (bf16[512,2048]{1,0:T(8,128)(2,1)S(1)}, s32[8,256]{1,0:T(8,128)}) custom-call(bf16[512,2048]{1,0:T(8,128)(2,1)} %ctx_ref.1, bf16[2048,8192]{1,0:T(8,128)(2,1)} %w_ref.1, bf16[1024,2048]{1,0:T(8,128)(2,1)} %bitcast.19, bf16[1024,2048]{1,0:T(8,128)(2,1)} %bitcast.21, s32[4,8,256]{2,1,0:T(8,128)} %concatenate.7.ids_out_ref, ...), custom_call_target="tpu_custom_call" | custom-call | flops 17179869184 | bytes 33554432 | tf_op jit(solution)/shard_map/pallas_call | solution.py:849
  180.5 1.2 slice.12
  182.4 1.3 copy.11
  (8 shorter events, 0.0 us)
